TPU v7x, 256 devices: a whole 4x4x8 slice. The times are simulated.
256 devices in a mesh: dp: 32 (over z_hi, x, core), tensor: 8 (over y, z_lo).
Axes of the slice: x: 4, y: 4, z: 8 (z_hi: 4, z_lo: 2; z = z_hi * 2 + z_lo), core: 2. Of those that a mesh axis runs over, the one named last changes fastest.
Arguments:
- query_acts: bfloat16 [1024, 5120], P(None, 'dp'), may hold values from -6 to 6
- query_pos: int32 [64], replicated, may hold values from 0 to 1023
- query_feat: int32 [64], replicated, may hold values from 0 to 127
- sae_enc: bfloat16 [128, 27648], P(None, 'tensor'), may hold values from -6 to 6
- basis_in: bfloat16 [5120, 5120], P('dp', 'tensor'), may hold values from -0.078125 to 0.078125
- basis_out: bfloat16 [27648, 27648], P('tensor', 'dp'), may hold values from -0.0390625 to 0.0390625
- eigvals: float32 [5120, 27648], P('tensor', 'dp'), may hold values from 0.05 to 900, as said below
- train_in: bfloat16 [32, 32, 5120], P('dp', None, 'tensor'), may hold values from -6 to 6
- train_out: bfloat16 [32, 32, 27648], P('dp'), may hold values from -6 to 6
Outputs:
- influence: float32 [64, 32], P(None, 'dp')
Inputs may be any that keep to these rules, and one draw needn't show every extreme that they name: eigvals are positive.
All inputs are finite; a program needn't handle non-finite values.
Results may differ from a plain program's by a relative error of at most 0.0075.
Values may be sent and summed in bfloat16 or wider, within the bound.
A program may use at most 128 MiB of HBM per device.

v0:
```python
import math

import jax
import jax.numpy as jnp
from jax import lax
from jax.sharding import PartitionSpec as P

DIN = 5120
DOUT = 27648
R = 32


damping = 0.1


def on_device(
    query_acts, query_pos, query_feat, sae_enc, basis_in, basis_out, eigvals, train_in, train_out
):
    context = query_acts.shape[0]
    picker = (query_pos[:, None] == jnp.arange(context)[None, :]).astype(jnp.bfloat16)
    inputs = jnp.dot(picker, query_acts, preferred_element_type=jnp.float32).astype(jnp.bfloat16)
    a_part = jnp.dot(inputs, basis_in, preferred_element_type=jnp.float32)
    a_eig, eig_dp = lax.psum((a_part, jnp.sum(eigvals)), "dp")
    monitored = sae_enc.shape[0]
    chooser = (query_feat[:, None] == jnp.arange(monitored)[None, :]).astype(jnp.bfloat16)
    outputs = jnp.dot(chooser, sae_enc, preferred_element_type=jnp.float32).astype(jnp.bfloat16)
    b_part = jnp.dot(outputs, basis_out, preferred_element_type=jnp.float32)
    b_sum, eig_total = lax.psum((b_part, eig_dp), "tensor")
    b_eig = b_sum.astype(jnp.bfloat16)
    inverse = 1.0 / (eigvals + damping * (eig_total / (DIN * DOUT)))
    left_all = lax.all_gather(train_in, "dp", axis=0, tiled=True)
    right_all = lax.all_to_all(train_out, "dp", split_axis=2, concat_axis=0, tiled=True)
    total_seqs = left_all.shape[0]
    block = math.gcd(total_seqs, 8)
    left_blocks = left_all.reshape((total_seqs // block, block) + left_all.shape[1:])
    right_blocks = right_all.reshape((total_seqs // block, block) + right_all.shape[1:])

    def per_block(pair):
        left, right = pair
        cross = jnp.einsum("bri,brj->bij", left, right, preferred_element_type=jnp.float32)
        damped = (cross * inverse[None]).astype(jnp.bfloat16)
        projected = jnp.einsum("bij,qj->bqi", damped, b_eig, preferred_element_type=jnp.float32)
        return jnp.sum(projected * a_eig[None], axis=2)

    partial_scores = lax.map(per_block, (left_blocks, right_blocks)).reshape(total_seqs, -1).T
    scale = 1.0 / math.sqrt(DIN * DOUT * R)
    owned = total_seqs // lax.axis_size("dp")
    summed = lax.psum(partial_scores, ("dp", "tensor"))
    result = lax.dynamic_slice_in_dim(summed, lax.axis_index("dp") * owned, owned, 1)
    return result * scale


def solution(mesh):
    in_specs = (
        P(None, "dp"),
        P(),
        P(),
        P(None, "tensor"),
        P("dp", "tensor"),
        P("tensor", "dp"),
        P("tensor", "dp"),
        P("dp", None, "tensor"),
        P("dp", None, None),
    )
    out_specs = P(None, "dp")
    return jax.shard_map(
        on_device, mesh=mesh, in_specs=in_specs, out_specs=out_specs, check_vma=False
    )
```

profile of v0, /device:TPU:1, one launch (start us, length us, event | category | flops | bytes accessed | tf_op | source)
XLA Modules:
  0.0 646.6 jit_solution(5923570678533881866)
XLA Ops:
  6.5 0.0 copy-start
  6.5 26.4 %copy.13 = bf16[1,32,27648]{1,0,2:T(2,128)(2,1)} copy(bf16[1,32,27648]{2,1,0:T(8,128)(2,1)} %param.19) | data formatting | bytes 3538944 | tf_op args[8]
  32.9 0.5 broadcast.4
  33.4 151.5 %reduce = bf16[27648,32]{1,0:T(8,128)(2,1)} reduce(bf16[27648,1,32]{2,1,0:T(2,128)(2,1)} %bitcast.42, bf16[]{:T(256)} %broadcast.4), dimensions={1}, to_apply=%bitcast.26.reduce_sub_computation | reduce | bytes 3538946
  184.9 8.9 %reshape.18 = bf16[32,2,13824]{2,1,0:T(2,128)(2,1)} reshape(bf16[27648,32]{1,0:T(8,128)(2,1)} %reduce) | data formatting | bytes 3538944
  193.8 12.8 %all-to-all-start = ((bf16[32,2,13824]{2,1,0:T(2,128)(2,1)}), bf16[32,2,13824]{2,1,0:T(2,128)(2,1)}, u32[]{:S(2)}, u32[]{:S(2)}) async-start(bf16[32,2,13824]{2,1,0:T(2,128)(2,1)} %reshape.18), calls=%async_computation | async-start | bytes 3538944 | tf_op jit(solution)/shard_map/all_to_all | solution.py:32
  206.6 0.0 copy-start.4
  206.6 0.0 all-reduce.4.cloned.1.call-start
  206.7 0.0 copy-done.2
  206.7 0.0 copy-done.3
  206.7 2.1 fusion.15
  208.8 0.0 all-reduce.4.cloned.1.call-update
  208.8 0.0 all-gather.2.cloned.1.call-start
  208.8 0.7 all-gather.2.cloned.1.call-update
  209.6 1.2 reduce_sum.18
  210.7 99.0 %psum.35 = f32[]{:T(128)} all-reduce(f32[]{:T(128)} %reduce_sum.18), channel_id=1, replica_groups=mesh['dp'=32,'tensor'=8] {'dp'}, use_global_device_ids=true, to_apply=%region_1.0 | all-reduce | flops 1 | bytes 8 | tf_op jit(solution)/shard_map/psum | solution.py:23
  309.7 4.7 fusion.14
  314.5 36.7 %all-reduce.5 = (f32[]{:T(128)}, bf16[64,864]{1,0:T(8,128)(2,1)S(1)}) all-reduce(f32[]{:T(128)} %psum.35, f32[64,864]{1,0:T(8,128)S(1)} %fusion.14), channel_id=1, replica_groups=mesh['dp'=32,'tensor'=8] {'tensor'}, use_global_device_ids=true, to_apply=%region_2.0 | all-reduce | flops 55297 | bytes 331784 | tf_op jit(solution)/shard_map/psum | solution.py:28
  351.9 1.6 add_divide_fusion
  353.5 0.0 all-to-all-done
  353.5 20.6 %reshape.19 = bf16[27648,1,32]{2,1,0:T(2,128)(2,1)} reshape(bf16[32,2,13824]{2,1,0:T(2,128)(2,1)} %all-to-all-done) | data formatting | bytes 3538944
  374.1 26.7 %copy.14 = bf16[1,32,27648]{2,1,0:T(8,128)(2,1)} copy(bf16[1,32,27648]{1,0,2:T(2,128)(2,1)} %bitcast.43) | data formatting | bytes 3538944 | tf_op jit(solution)/shard_map/all_to_all | solution.py:32
  400.8 3.9 all_to_all.12
  404.7 79.8 %all-reduce.4.cloned.1.call-done = f32[64,640]{1,0:T(8,128)} async-done(((f32[64,640]{1,0:T(8,128)}), f32[64,640]{1,0:T(8,128)}) %all-reduce.4.cloned.1.call-update) | async-done | bytes 163856 | tf_op jit(solution)/shard_map/psum | solution.py:23
  484.5 56.3 %all-gather.2.cloned.1.call-done = bf16[32,32,640]{2,1,0:T(8,128)(2,1)} async-done(((bf16[1,32,640]{2,1,0:T(8,128)(2,1)}), bf16[32,32,640]{2,1,0:T(8,128)(2,1)}) %all-gather.2.cloned.1.call-update) | async-done | bytes 1310736 | tf_op jit(solution)/shard_map/all_gather | solution.py:31
  540.8 23.7 %while.10 = (s32[]{:T(128)}, f32[4,8,64]{2,1,0:T(8,128)S(1)}, bf16[4,8,32,640]{3,2,1,0:T(8,128)(2,1)}, bf16[4,8,32,864]{3,1,0,2:T(8,128)(2,1)S(1)}, f32[640,864]...) while((s32[]{:T(128)}, f32[4,8,64]{2,1,0:T(8,128)S(1)}, ...), condition=%wide.region_7.8_spmd, body=%wide.region_5.7_spmd.sunk | while | flops 858848768 | bytes 4151401 | solution.py:45
  540.9 5.8 fusion.29
  546.8 5.9 fusion.29
  552.7 5.9 fusion.29
  558.7 5.9 fusion.29
  564.6 74.7 %psum.39 = f32[64,32]{0,1:T(8,128)S(1)} all-reduce(f32[64,32]{0,1:T(8,128)S(1)} %bitcast.45), channel_id=1, replica_groups=mesh['dp'=32,'tensor'=8] {'dp','tensor'}, use_global_device_ids=true, to_apply=%region_8.9 | all-reduce | flops 2048 | bytes 16384 | tf_op jit(solution)/shard_map/psum | solution.py:48
  639.3 0.5 dynamic-slice_multiply_fusion
  (15 shorter events, 0.2 us)
Async XLA Ops:
  6.5 303.2 %copy-start = (bf16[128,3456]{1,0:T(8,128)(2,1)S(1)}, bf16[128,3456]{1,0:T(8,128)(2,1)}, u32[]{:S(2)}) copy-start(bf16[128,3456]{1,0:T(8,128)(2,1)} %param.14) | copy-start | bytes 2654212
  193.8 12.9 %copy-start.2 = (bf16[1024,160]{0,1:T(8,128)(2,1)S(1)}, bf16[1024,160]{0,1:T(8,128)(2,1)}, u32[]{:S(2)}) copy-start(bf16[1024,160]{0,1:T(8,128)(2,1)} %param.11) | copy-start | bytes 983044
  193.8 12.9 %copy-start.3 = (s32[64]{0:T(128)S(1)}, s32[64]{0:T(128)}, u32[]{:S(2)}) copy-start(s32[64]{0:T(128)} %param.12) | copy-start | bytes 772
  193.8 15.7 %copy-start.1 = (f32[640,864]{0,1:T(8,128)S(1)}, f32[640,864]{0,1:T(8,128)}, u32[]{:S(2)}) copy-start(f32[640,864]{0,1:T(8,128)} %param.17) | copy-start | bytes 6635524
  193.8 159.7 %all-to-all-start = ((bf16[32,2,13824]{2,1,0:T(2,128)(2,1)}), bf16[32,2,13824]{2,1,0:T(2,128)(2,1)}, u32[]{:S(2)}, u32[]{:S(2)}) async-start(bf16[32,2,13824]{2,1,0:T(2,128)(2,1)} %reshape.18), calls=%async_computation | async-start | bytes 3538944 | tf_op jit(solution)/shard_map/all_to_all | solution.py:32
  206.6 103.1 %copy-start.4 = (s32[64]{0:T(128)S(1)}, s32[64]{0:T(128)}, u32[]{:S(2)}) copy-start(s32[64]{0:T(128)} %param.13) | copy-start | bytes 772
  206.6 277.8 %all-reduce.4.cloned.1.call-start = ((), (), s32[]{:S(2)}) async-start(), calls=%async_computation.2 | async-start | bytes 327680 | tf_op jit(solution)/shard_map/psum | solution.py:23
  208.8 332.0 %all-gather.2.cloned.1.call-start = ((), (), s32[]{:S(2)}) async-start(), calls=%async_computation.1 | async-start | bytes 1351680 | tf_op jit(solution)/shard_map/all_gather | solution.py:31
Sparse Core Ops, SparseCore 0:
  210.1 274.3 all-reduce.3
  487.4 53.4 all-gather.1
where the time goes:
time: 652 us; the launch traced here: 647 us
  blocking collectives  210 us (32%)
  other arithmetic  155 us (24%)
  waiting for transfers between devices  137 us (21%)
  local copies, waits for them, and re-layouts  87.2 us (13%)
  matrix products  30.2 us (5%)
  between operations  14.1 us (2%)
  starting transfers between devices  12.9 us (2%)
    unnamed x1, other arithmetic  151 us
    psum x1, blocking collectives, on_device(): a_eig, eig_dp = lax.psum((a_part, jnp.sum(eigvals)), 'dp')  99 us
    psum x1, waiting for transfers between devices, on_device(): a_eig, eig_dp = lax.psum((a_part, jnp.sum(eigvals)), 'dp')  79.8 us
    psum x1, blocking collectives, on_device(): summed = lax.psum(partial_scores, ('dp', 'tensor'))  74.7 us
    unnamed x14, local copies, waits for them, and re-layouts  56.4 us
    all_gather x1, waiting for transfers between devices, on_device(): left_all = lax.all_gather(train_in, 'dp', axis=0, tiled=True)  56.3 us
    psum x1, blocking collectives, on_device(): b_sum, eig_total = lax.psum((b_part, eig_dp), 'tensor')  36.7 us
    all_to_all x2, local copies, waits for them, and re-layouts, on_device(): lax.all_to_all(train_out, 'dp', split_axis=2, concat_axis=0, tiled=True)  30.6 us
  transfers between devices with their start and end apart: 3, of which 2 were waited for; matrix products, arithmetic and copies ran while one was open for 9% of the time, Pallas kernels for 0%

commit v1 on v0

v1 whole, which is shorter than its diff:
```python
import math

import jax
import jax.numpy as jnp
from jax import lax
from jax.experimental import pallas as pl
from jax.experimental.pallas import tpu as pltpu
from jax.sharding import PartitionSpec as P

DIN = 5120
DOUT = 27648
R = 32
damping = 0.1

ZH, X, CORE, Y, ZL = 4, 4, 2, 4, 2
XC = X * CORE
DP = ZH * XC
TENSOR = Y * ZL
SEQS = 32
Q = 64
I = DIN // TENSOR
J = DOUT // DP
JP = 1024
MESH = pl.DeviceIdType.MESH
f32 = jnp.float32
bf16 = jnp.bfloat16
FIRST_ROWS = (((0,), (0,)), ((), ()))


def kernel(
    pos_ref, feat_ref, acts_hbm, sae_hbm, bin_hbm, bout_hbm, eig_hbm, tin_hbm, tout_hbm,
    out_ref,
    acts, sae, bin_, bout, eig, tout, inv, right_out, right, left,
    b_part, b_recv, b_sum, b_all, b_lo,
    e_sum, e_xc, e_mid, e_z,
    a_part, a_xc, a_mid, a_z, a_sum, a_all, a_full,
    damped, scores, f_part, f_z, f_mid, f_xc, f_last, f_t,
    local_sem, r_send, r_recv, y_send, y_again, lz_send, lz_recv, lx_send, lx_recv, lc_send, lc_recv,
    b_send, b_rsem, bg_send, bg_recv, e_send, e_recv, ez_send, ez_recv,
    a_send, a_recv, az_send, az_recv, ag_send, ag_recv,
    fz_send, fz_recv, fx_send, fx_recv, ft_send, ft_recv,
):
    d = lax.axis_index("dp")
    t = lax.axis_index("tensor")
    zh, xc = lax.div(d, XC), lax.rem(d, XC)
    x, core = lax.div(xc, CORE), lax.rem(xc, CORE)
    y, zl = lax.div(t, ZL), lax.rem(t, ZL)

    def remote(src, dst, send, recv, dp, tensor):
        return pltpu.make_async_remote_copy(
            src_ref=src, dst_ref=dst, send_sem=send, recv_sem=recv,
            device_id={"dp": dp, "tensor": tensor}, device_id_type=MESH,
        )

    def others(count, me, body):
        def step(k, carry):
            body(lax.rem(me + k, count))
            return carry

        lax.fori_loop(1, count, step, 0)

    def spread(count, me, src, dst, send, recv, place):
        def body(o):
            dp, tensor = place(o)
            remote(src(o), dst.at[me], send.at[o], recv.at[me], dp, tensor).start()

        others(count, me, body)

    def collect(count, me, src, dst, send, recv):
        def body(o):
            remote(src(o), dst.at[o], send.at[o], recv.at[o], d, t).wait_recv()

        others(count, me, body)

    def drain(count, me, src, dst, send, recv):
        def body(o):
            remote(src(o), dst.at[me], send.at[o], recv.at[me], d, t).wait_send()

        others(count, me, body)

    in_xc = lambda o: (zh * XC + o, t)
    in_zh = lambda o: (o * XC + xc, t)
    in_t = lambda o: (d, o)
    in_dp = lambda o: (o, t)

    loads = [
        pltpu.make_async_copy(src, dst, local_sem.at[n])
        for n, (src, dst) in enumerate((
            (tout_hbm, tout), (tin_hbm, left.at[zh, x, core]), (eig_hbm, eig), (sae_hbm, sae),
            (bout_hbm, bout), (acts_hbm, acts), (bin_hbm, bin_),
        ))
    ]
    for load in loads:
        load.start()
    l_tout, l_tin, l_eig, l_sae, l_bout, l_acts, l_bin = loads

    barrier = pltpu.get_barrier_semaphore()

    def greet_dp(o):
        pl.semaphore_signal(barrier, inc=1, device_id={"dp": o, "tensor": t}, device_id_type=MESH)

    def greet_t(o):
        pl.semaphore_signal(barrier, inc=1, device_id={"dp": d, "tensor": o}, device_id_type=MESH)

    others(DP, d, greet_dp)
    others(TENSOR, t, greet_t)

    is_source = lax.rem(x + zh + 2 * core + zl, Y) == y

    l_tout.wait()

    @pl.when(is_source)
    def _():
        def four(g, carry):
            wide = tout[:, pl.ds(pl.multiple_of(g * (4 * J), 128), 4 * J)]
            for p in range(4):
                right_out[g * 4 + p] = wide[:, p * J:(p + 1) * J]
            return carry

        lax.fori_loop(0, DP // 4, four, 0)

    l_tin.wait()
    pl.semaphore_wait(barrier, DP + TENSOR - 2)

    def left_z(o):
        remote(left.at[zh, x, core], left.at[zh, x, core], lz_send.at[o], lz_recv.at[zh],
               o * XC + xc, t).start()

    others(ZH, zh, left_z)

    @pl.when(is_source)
    def _():
        pltpu.make_async_copy(right_out.at[d], right.at[d], r_recv.at[d]).start()

        def send(o):
            remote(right_out.at[o], right.at[d], r_send.at[o], r_recv.at[d], o, t).start()

        others(DP, d, send)

    l_eig.wait()
    folded = jnp.sum(eig[...].reshape(I // 8, 8, J), axis=0)
    e_part = jnp.concatenate([folded[:, 768:], jnp.zeros((8, 32), f32)], axis=1)
    for n in range(6):
        e_part = e_part + folded[:, n * 128:(n + 1) * 128]

    l_sae.wait()
    monitored = sae.shape[0]
    chooser = jnp.where(
        lax.broadcasted_iota(jnp.int32, (monitored, Q), 0) == feat_ref[...], 1.0, 0.0
    ).astype(bf16)
    outputs = lax.dot_general(chooser, sae[...], FIRST_ROWS, preferred_element_type=f32).astype(bf16)
    l_bout.wait()
    b_mine = jnp.dot(outputs, bout[...], preferred_element_type=f32)
    for n in range(TENSOR):
        b_part[n, :, 0:J] = b_mine[8 * n:8 * (n + 1)]
        b_part[n, :, 896:JP] = e_part
    spread(TENSOR, t, lambda o: b_part.at[o], b_recv, b_send, b_rsem, in_t)
    b_recv[t] = b_part[t]

    def left_z_wait(o):
        remote(left.at[o, x, core], left.at[o, x, core], lz_send.at[o], lz_recv.at[o], d, t).wait_recv()

    others(ZH, zh, left_z_wait)

    def left_x(o):
        remote(left.at[:, x, core], left.at[:, x, core], lx_send.at[o], lx_recv.at[x],
               zh * XC + o * CORE + core, t).start()

    others(X, x, left_x)

    def left_core(o):
        remote(left.at[:, o, core], left.at[:, o, core], lc_send.at[o], lc_recv.at[o],
               zh * XC + x * CORE + (1 - core), t).start()

    left_core(x)

    l_acts.wait()
    context = acts.shape[0]
    picker = jnp.where(
        lax.broadcasted_iota(jnp.int32, (context, Q), 0) == pos_ref[...], 1.0, 0.0
    ).astype(bf16)
    inputs = lax.dot_general(picker, acts[...], FIRST_ROWS, preferred_element_type=f32).astype(bf16)
    l_bin.wait()
    a_mine = jnp.dot(inputs, bin_[...], preferred_element_type=f32)
    for n in range(XC):
        a_part[n] = a_mine[8 * n:8 * (n + 1)]
    spread(XC, xc, lambda o: a_part.at[o], a_xc, a_send, a_recv, in_xc)
    a_xc[xc] = a_part[xc]

    collect(TENSOR, t, lambda o: b_part.at[o], b_recv, b_send, b_rsem)
    total = b_recv[0]
    for n in range(1, TENSOR):
        total = total + b_recv[n]
    b_sum[...] = total[:, 0:896]
    e_sum[...] = total[:, 896:JP]
    spread(XC, xc, lambda o: e_sum, e_xc, e_send, e_recv, in_xc)
    spread(TENSOR, t, lambda o: b_sum, b_all, bg_send, bg_recv, in_t)
    e_xc[xc] = e_sum[...]
    b_all[t] = b_sum[...]

    for n in range(I // 128):
        inv[:, n * 128:(n + 1) * 128] = eig[n * 128:(n + 1) * 128, :].T

    def left_x_wait(o):
        remote(left.at[:, o, core], left.at[:, o, core], lx_send.at[o], lx_recv.at[o], d, t).wait_recv()
        left_core(o)

    others(X, x, left_x_wait)

    collect(XC, xc, lambda o: e_sum, e_xc, e_send, e_recv)
    total = e_xc[0]
    for n in range(1, XC):
        total = total + e_xc[n]
    e_mid[...] = total
    spread(ZH, zh, lambda o: e_mid, e_z, ez_send, ez_recv, in_zh)
    e_z[zh] = e_mid[...]

    collect(XC, xc, lambda o: a_part.at[o], a_xc, a_send, a_recv)
    total = a_xc[0]
    for n in range(1, XC):
        total = total + a_xc[n]
    a_mid[...] = total
    spread(ZH, zh, lambda o: a_mid, a_z, az_send, az_recv, in_zh)
    a_z[zh] = a_mid[...]

    collect(TENSOR, t, lambda o: b_sum, b_all, bg_send, bg_recv)
    for n in range(TENSOR // 2):
        pair = jnp.concatenate([b_all[2 * n], b_all[2 * n + 1]], axis=0)
        b_lo[16 * n:16 * (n + 1), :] = pair.astype(bf16)[:, 0:J]

    collect(ZH, zh, lambda o: a_mid, a_z, az_send, az_recv)
    a_sum[...] = ((a_z[0] + a_z[1]) + (a_z[2] + a_z[3])) * (1.0 / math.sqrt(DIN * DOUT * R))
    spread(XC, xc, lambda o: a_sum, a_all, ag_send, ag_recv, in_xc)
    a_all[xc] = a_sum[...]

    collect(ZH, zh, lambda o: e_mid, e_z, ez_send, ez_recv)
    eig_total = jnp.sum((e_z[0] + e_z[1]) + (e_z[2] + e_z[3]))
    shift = damping * (eig_total / (DIN * DOUT))

    def invert(n, carry):
        rows = pl.ds(pl.multiple_of(n * 96, 8), 96)
        inv[rows, :] = 1.0 / (inv[rows, :] + shift)
        return carry

    lax.fori_loop(0, J // 96, invert, 0)

    def seq_of(k):
        g, m = lax.div(k, 8), lax.rem(k, 8)
        low = m < 4
        off = jnp.where(g == 0, 0, jnp.where(g == 3, 2, jnp.where((g == 1) == low, 1, 3)))
        plane = lax.rem(y + off, Y)
        sz, sc = lax.div(m, CORE), lax.rem(m, CORE)
        sx = lax.rem(plane - sz - 2 * sc - zl + 2 * Y, Y)
        return sz, sx, sc

    def flat(s):
        return (s[0] * X + s[1]) * CORE + s[2]

    def right_wait(s):
        remote(right.at[s], right.at[s], y_again.at[0], r_recv.at[s], d, t).wait_recv()

    def to_plane(s, off, sem):
        return remote(right.at[s], right.at[s], sem, r_recv.at[s], d, lax.rem(y + off, Y) * ZL + zl)

    def own(m, carry):
        s = flat(seq_of(m))
        right_wait(s)
        to_plane(s, 1, y_send.at[0, m]).start()
        to_plane(s, 3, y_send.at[1, m]).start()
        return carry

    lax.fori_loop(0, 8, own, 0)

    def left_core_wait(o, carry):
        remote(left.at[:, o, 1 - core], left.at[:, o, 1 - core], lc_send.at[o], lc_recv.at[o], d, t).wait_recv()
        return carry

    lax.fori_loop(0, X, left_core_wait, 0)

    collect(XC, xc, lambda o: a_sum, a_all, ag_send, ag_recv)
    for n in range(XC):
        a_full[8 * n:8 * (n + 1), :] = a_all[n]

    def ready(k):
        @pl.when(k >= 8)
        def _():
            s = flat(seq_of(k))
            right_wait(s)

            @pl.when(k < 16)
            def _():
                m = k - 8
                to_plane(s, jnp.where(m < 4, 3, 1), y_again.at[m]).start()

    def cross(k, slot):
        s = seq_of(k)
        wide = lax.dot_general(
            right[flat(s)], left[s[0], s[1], s[2]], FIRST_ROWS, preferred_element_type=f32
        )
        damped[slot] = (wide * inv[...]).astype(bf16)

    def project(k, slot):
        s = flat(seq_of(k))
        part = jnp.dot(b_lo[...], damped[slot], preferred_element_type=f32) * a_full[...]
        row = part[:, 0:128]
        for n in range(1, I // 128):
            row = row + part[:, n * 128:(n + 1) * 128]
        row = jnp.sum(row, axis=1, keepdims=True)
        lane = lax.broadcasted_iota(jnp.int32, (Q, 128), 1)
        scores[...] = jnp.where(lane == s, row, scores[...])

    scores[...] = jnp.zeros_like(scores)
    cross(0, 0)

    def two(h, carry):
        k = 2 * h
        ready(k + 1)
        cross(k + 1, 1)
        project(k, 0)
        ready(k + 2)
        cross(k + 2, 0)
        project(k + 1, 1)
        return carry

    lax.fori_loop(0, SEQS // 2 - 1, two, 0)
    ready(SEQS - 1)
    cross(SEQS - 1, 1)
    project(SEQS - 2, 0)
    project(SEQS - 1, 1)

    rows = scores[...].T
    for n in range(ZH):
        f_part[n, :, 0:Q] = rows[8 * n:8 * (n + 1), :]
        f_part[n, :, Q:128] = jnp.zeros((8, 128 - Q), f32)
    spread(ZH, zh, lambda o: f_part.at[o], f_z, fz_send, fz_recv, in_zh)
    f_z[zh] = f_part[zh]
    collect(ZH, zh, lambda o: f_part.at[o], f_z, fz_send, fz_recv)
    f_mid[...] = (f_z[0] + f_z[1]) + (f_z[2] + f_z[3])
    spread(XC, xc, lambda o: f_mid, f_xc, fx_send, fx_recv, in_xc)
    f_xc[xc] = f_mid[...]
    collect(XC, xc, lambda o: f_mid, f_xc, fx_send, fx_recv)
    total = f_xc[0]
    for n in range(1, XC):
        total = total + f_xc[n]
    f_last[...] = total
    spread(TENSOR, t, lambda o: f_last, f_t, ft_send, ft_recv, in_t)
    f_t[t] = f_last[...]

    @pl.when(is_source)
    def _():
        def sent(o):
            remote(right_out.at[o], right.at[d], r_send.at[o], r_recv.at[d], o, t).wait_send()

        others(DP, d, sent)

    def sent_y(m, carry):
        to_plane(0, 1, y_send.at[0, m]).wait_send()
        to_plane(0, 1, y_send.at[1, m]).wait_send()
        to_plane(0, 1, y_again.at[m]).wait_send()
        return carry

    lax.fori_loop(0, 8, sent_y, 0)
    drain(TENSOR, t, lambda o: b_part.at[o], b_recv, b_send, b_rsem)
    drain(TENSOR, t, lambda o: b_sum, b_all, bg_send, bg_recv)
    drain(XC, xc, lambda o: e_sum, e_xc, e_send, e_recv)
    drain(ZH, zh, lambda o: e_mid, e_z, ez_send, ez_recv)
    drain(XC, xc, lambda o: a_part.at[o], a_xc, a_send, a_recv)
    drain(ZH, zh, lambda o: a_mid, a_z, az_send, az_recv)
    drain(XC, xc, lambda o: a_sum, a_all, ag_send, ag_recv)
    drain(ZH, zh, lambda o: f_part.at[o], f_z, fz_send, fz_recv)
    drain(XC, xc, lambda o: f_mid, f_xc, fx_send, fx_recv)

    def sent_left_z(o):
        remote(left.at[zh, x, core], left.at[zh, x, core], lz_send.at[o], lz_recv.at[zh], d, t).wait_send()

    others(ZH, zh, sent_left_z)

    def sent_left_x(o):
        remote(left.at[:, x, core], left.at[:, x, core], lx_send.at[o], lx_recv.at[x], d, t).wait_send()

    others(X, x, sent_left_x)

    def sent_left_core(o, carry):
        remote(left.at[:, o, core], left.at[:, o, core], lc_send.at[o], lc_recv.at[o], d, t).wait_send()
        return carry

    lax.fori_loop(0, X, sent_left_core, 0)

    collect(TENSOR, t, lambda o: f_last, f_t, ft_send, ft_recv)
    total = f_t[0]
    for n in range(1, TENSOR):
        total = total + f_t[n]
    f_last_row = jnp.sum(
        jnp.where(lax.broadcasted_iota(jnp.int32, (8, 128), 0) == xc, total, 0.0), axis=0, keepdims=True
    )
    out_ref[...] = jnp.broadcast_to(f_last_row, (8, 128)).T[0:Q, 0:1]
    drain(TENSOR, t, lambda o: f_last, f_t, ft_send, ft_recv)


def on_device(
    query_acts, query_pos, query_feat, sae_enc, basis_in, basis_out, eigvals, train_in, train_out
):
    context = query_acts.shape[0]
    monitored = sae_enc.shape[0]
    vmem = pltpu.VMEM
    dma = pltpu.SemaphoreType.DMA
    scratch = [
        vmem((context, DIN // DP), bf16), vmem((monitored, DOUT // TENSOR), bf16),
        vmem((DIN // DP, I), bf16), vmem((DOUT // TENSOR, J), bf16), vmem((I, J), f32),
        vmem((R, DOUT), bf16), vmem((J, I), f32),
        vmem((DP, R, J), bf16), vmem((SEQS, R, J), bf16), vmem((ZH, X, CORE, R, I), bf16),
        vmem((TENSOR, 8, JP), f32), vmem((TENSOR, 8, JP), f32), vmem((8, 896), f32),
        vmem((TENSOR, 8, 896), f32), vmem((Q, J), bf16),
        vmem((8, 128), f32), vmem((XC, 8, 128), f32), vmem((8, 128), f32), vmem((ZH, 8, 128), f32),
        vmem((XC, 8, I), f32), vmem((XC, 8, I), f32), vmem((8, I), f32), vmem((ZH, 8, I), f32),
        vmem((8, I), f32), vmem((XC, 8, I), f32), vmem((Q, I), f32),
        vmem((2, J, I), bf16), vmem((Q, 128), f32),
        vmem((ZH, 8, 128), f32), vmem((ZH, 8, 128), f32), vmem((8, 128), f32),
        vmem((XC, 8, 128), f32), vmem((8, 128), f32), vmem((TENSOR, 8, 128), f32),
        dma((7,)), dma((DP,)), dma((SEQS,)), dma((2, 8)), dma((8,)),
        dma((ZH,)), dma((ZH,)), dma((X,)), dma((X,)), dma((X,)), dma((X,)),
        dma((TENSOR,)), dma((TENSOR,)), dma((TENSOR,)), dma((TENSOR,)),
        dma((XC,)), dma((XC,)), dma((ZH,)), dma((ZH,)),
        dma((XC,)), dma((XC,)), dma((ZH,)), dma((ZH,)), dma((XC,)), dma((XC,)),
        dma((ZH,)), dma((ZH,)), dma((XC,)), dma((XC,)), dma((TENSOR,)), dma((TENSOR,)),
    ]
    anywhere = pl.BlockSpec(memory_space=pl.ANY)
    inside = pl.BlockSpec(memory_space=pltpu.VMEM)
    return pl.pallas_call(
        kernel,
        out_shape=jax.ShapeDtypeStruct((Q, 1), f32),
        in_specs=[inside, inside] + [anywhere] * 7,
        out_specs=inside,
        scratch_shapes=scratch,
        compiler_params=pltpu.CompilerParams(
            collective_id=0, has_side_effects=True, vmem_limit_bytes=56 << 20
        ),
        name="influence",
    )(
        query_pos.reshape(1, Q), query_feat.reshape(1, Q), query_acts, sae_enc, basis_in, basis_out,
        eigvals, train_in.reshape(R, I), train_out.reshape(R, DOUT),
    )


def solution(mesh):
    in_specs = (
        P(None, "dp"),
        P(),
        P(),
        P(None, "tensor"),
        P("dp", "tensor"),
        P("tensor", "dp"),
        P("tensor", "dp"),
        P("dp", None, "tensor"),
        P("dp", None, None),
    )
    out_specs = P(None, "dp")
    return jax.shard_map(
        on_device, mesh=mesh, in_specs=in_specs, out_specs=out_specs, check_vma=False
    )
```

time: 652 us -> 103 us (0.16)
  blocking collectives: 210 us -> 0 us
  other arithmetic: 155 us -> 0 us
  waiting for transfers between devices: 137 us -> 0 us
  Pallas kernels: 0 us -> 87.1 us
  local copies, waits for them, and re-layouts: 87.2 us -> 15.7 us
  matrix products: 30.2 us -> 0 us
  between operations: 14.1 us -> 0.01 us
  starting transfers between devices: 12.9 us -> 0 us
    psum x3 -> x0, blocking collectives: 210 us -> none  [the longest x1 99 us: on_device(): a_eig, eig_dp = lax.psum((a_part, jnp.sum(eigvals)), 'dp')]
    unnamed x1 -> x0, other arithmetic: 151 us -> none
    pallas_call x0 -> x1, Pallas kernels: none -> 87.1 us  [on_device(): pl.pallas_call(kernel, out_shape=jax.ShapeDtypeStruct((Q, 1), f32), in_sp...]
    psum x1 -> x0, waiting for transfers between devices: 79.8 us -> none  [on_device(): a_eig, eig_dp = lax.psum((a_part, jnp.sum(eigvals)), 'dp')]
    all_gather x1 -> x0, waiting for transfers between devices: 56.3 us -> none  [on_device(): left_all = lax.all_gather(train_in, 'dp', axis=0, tiled=True)]
    unnamed x14 -> x3, local copies, waits for them, and re-layouts: 56.4 us -> 14.4 us
    all_to_all x2 -> x0, local copies, waits for them, and re-layouts: 30.6 us -> none  [on_device(): lax.all_to_all(train_out, 'dp', split_axis=2, concat_axis=0, tiled=True)]
    dot_general x6 -> x0, matrix products: 30.2 us -> none  [the longest x4 23.4 us: per_block(): jnp.einsum('bij,qj->bqi', damped, b_eig, preferred_element_type=jnp.float32)]
  transfers between devices with their start and end apart: 3 -> 0, of which waited for: 2 -> 0; matrix products, arithmetic and copies ran while one was open for 9% -> 0% of each run, Pallas kernels for 0% -> 0%
where the time goes in v1:
time: 103 us
  Pallas kernels  87.1 us (85%)
  local copies, waits for them, and re-layouts  15.7 us (15%)
    pallas_call x1, Pallas kernels, on_device(): pl.pallas_call(kernel, out_shape=jax.ShapeDtypeStruct((Q, 1), f32), in_sp...  87.1 us
    unnamed x3, local copies, waits for them, and re-layouts  14.4 us

profile of v1, /device:TPU:1, one launch (start us, length us, event | category | flops | bytes accessed | tf_op | source)
XLA Modules:
  0.0 102.8 jit_solution(10196785851868228203)
XLA Ops:
  0.0 2.0 %copy.10.acts_hbm = bf16[1024,160]{1,0:T(8,128)(2,1)} copy(bf16[1024,160]{0,1:T(8,128)(2,1)} %param.9) | data formatting | bytes 655360 | tf_op args[0]
  2.0 3.2 %copy.12.eig_hbm = f32[640,864]{1,0:T(8,128)} copy(f32[640,864]{0,1:T(8,128)} %param.15) | data formatting | bytes 4423680 | tf_op args[6]
  5.2 9.2 %copy.11.bout_hbm = bf16[3456,864]{1,0:T(8,128)(2,1)} copy(bf16[3456,864]{0,1:T(8,128)(2,1)} %param.14) | data formatting | bytes 11943936 | tf_op args[5]
  14.4 87.1 %influence.1 = f32[64,1]{1,0:T(8,128)} custom-call(s32[1,64]{1,0:T(1,128)} %bitcast.6, s32[1,64]{1,0:T(1,128)} %bitcast.7, bf16[1024,160]{1,0:T(8,128)(2,1)} %copy.10.acts_hbm, bf16[128,3456]{1,0:T(8,128)(2,1)} %sae_hbm.1, bf16[160,640]{1,0:T(8,128)(2,1)} %bin_hbm.1, bf16[3456,864]{1,0:T(8,128)(2,1)} %copy.11.bout_hbm, f32[640,864]{1,0:T(8,128)} %copy.12.eig_hbm, ...), custom_call_target="tpu_custom_call" | custom-call | tf_op jit(solution)/shard_map/influence/pallas_call | solution.py:429
  101.4 1.3 %copy.13 = f32[64,1]{0,1:T(1,128)} copy(f32[64,1]{1,0:T(8,128)} %influence.1) | data formatting | bytes 512 | tf_op jit(solution)/shard_map/influence/pallas_call | solution.py:429

commit v2 on v1

v2 whole, which is shorter than its diff:
```python
import math

import jax
import jax.numpy as jnp
from jax import lax
from jax.experimental import pallas as pl
from jax.experimental.pallas import tpu as pltpu
from jax.sharding import PartitionSpec as P

DIN = 5120
DOUT = 27648
R = 32
damping = 0.1

ZH, X, CORE, Y, ZL = 4, 4, 2, 4, 2
XC = X * CORE
DP = ZH * XC
TENSOR = Y * ZL
SEQS = 32
Q = 64
I = DIN // TENSOR
J = DOUT // DP
JP = 896
MESH = pl.DeviceIdType.MESH
f32 = jnp.float32
bf16 = jnp.bfloat16
FIRST_ROWS = (((0,), (0,)), ((), ()))
LAST_COLUMNS = (((1,), (1,)), ((), ()))


def wrap(v, n):
    return jnp.where(v >= n, v - n, v)


def half_of(v):
    return jnp.where(v >= 4, jnp.where(v >= 6, 3, 2), jnp.where(v >= 2, 1, 0))


def kernel(
    pos_ref, feat_ref, acts_hbm, sae_hbm, bin_hbm, bout_hbm, eig_hbm, tin_hbm, tout_hbm,
    out_ref,
    acts, sae, bin_, bout, inv, tout, right_out, right_row, right, left,
    b_mine, b_part, b_recv, b_sum, b_all, b_lo,
    e_mine, e_z, e_sum, e_xc, e_mid, e_t,
    a_part, a_xc, a_mid, a_z, a_sum, a_all, a_full,
    damped, rows, scores, f_part, f_z, f_mid, f_xc, f_last, f_t,
    local_sem, rz_send, rz_recv, r_send, r_recv, y_send, y_again, lz_send, lz_recv, lx_send, lx_recv, lc_send, lc_recv,
    b_send, b_rsem, bg_send, bg_recv, ez_send, ez_recv, e_send, e_recv, et_send, et_recv,
    a_send, a_recv, az_send, az_recv, ag_send, ag_recv,
    fz_send, fz_recv, fx_send, fx_recv, ft_send, ft_recv,
):
    d = lax.axis_index("dp")
    t = lax.axis_index("tensor")
    zh, xc = lax.div(d, XC), lax.rem(d, XC)
    x, core = lax.div(xc, CORE), lax.rem(xc, CORE)
    y, zl = lax.div(t, ZL), lax.rem(t, ZL)

    def remote(src, dst, send, recv, dp, tensor):
        return pltpu.make_async_remote_copy(
            src_ref=src, dst_ref=dst, send_sem=send, recv_sem=recv,
            device_id={"dp": dp, "tensor": tensor}, device_id_type=MESH,
        )

    def total_of(ref, count):
        total = ref[0]
        for n in range(1, count):
            total = total + ref[n]
        return total

    def others(count, me, body):
        def step(k, carry):
            body(wrap(me + k, count))
            return carry

        lax.fori_loop(1, count, step, 0)

    def spread(count, me, src, dst, send, recv, place):
        def body(o):
            dp, tensor = place(o)
            remote(src(o), dst.at[me], send.at[o], recv.at[me], dp, tensor).start()

        others(count, me, body)

    def collect(count, me, src, dst, send, recv):
        def body(o):
            remote(src(o), dst.at[o], send.at[o], recv.at[o], d, t).wait_recv()

        others(count, me, body)

    def drain(count, me, src, dst, send, recv):
        def body(o):
            remote(src(o), dst.at[me], send.at[o], recv.at[me], d, t).wait_send()

        others(count, me, body)

    in_xc = lambda o: (zh * XC + o, t)
    in_zh = lambda o: (o * XC + xc, t)
    in_t = lambda o: (d, o)

    loads = [
        pltpu.make_async_copy(src, dst, local_sem.at[n])
        for n, (src, dst) in enumerate((
            (tout_hbm, tout), (tin_hbm, left.at[zh, x, core]), (eig_hbm, inv), (acts_hbm, acts), (bin_hbm, bin_),
            (sae_hbm, sae), (bout_hbm, bout),
        ))
    ]
    for load in loads:
        load.start()
    l_tout, l_tin, l_eig, l_acts, l_bin, l_sae, l_bout = loads

    barrier = pltpu.get_barrier_semaphore()

    def greet(place):
        def body(o):
            dp, tensor = place(o)
            pl.semaphore_signal(barrier, inc=1, device_id={"dp": dp, "tensor": tensor}, device_id_type=MESH)

        return body

    others(ZH, zh, greet(in_zh))
    others(TENSOR, t, greet(in_t))
    others(XC, xc, greet(in_xc))

    def low_two(v):
        return wrap(wrap(v, 8), 4)

    hop = low_two(x + 2 * core + zl - y + Y)
    row = wrap(zh + hop, ZH)
    column_seq = wrap(zh - hop + ZH, ZH) * XC + xc

    l_tout.wait()

    def four(half, carry):
        wide = tout[:, pl.ds(pl.multiple_of((2 * row + half) * (4 * J), 128), 4 * J)]
        for p in range(4):
            right_out[half * 4 + p, :, 0:J] = wide[:, p * J:(p + 1) * J]
        return carry

    lax.fori_loop(0, 2, four, 0)

    l_eig.wait()

    def fold(n, total):
        some = inv[pl.ds(pl.multiple_of(n * 96, 8), 96), :]
        some = jnp.sum(some.reshape(12, 8, I), axis=0)
        for c in range(I // 128):
            total = total + some[:, c * 128:(c + 1) * 128]
        return total

    e_part = lax.fori_loop(0, J // 96, fold, jnp.zeros((8, 128), f32))
    e_mine[...] = e_part
    e_z[zh] = e_part
    l_tin.wait()

    pl.semaphore_wait(barrier, ZH + TENSOR + XC - 3)
    spread(ZH, zh, lambda o: e_mine, e_z, ez_send, ez_recv, in_zh)

    def left_z(o):
        return remote(left.at[zh, x, core], left.at[zh, x, core], lz_send.at[o], lz_recv.at[zh],
                      o * XC + xc, t)

    others(ZH, zh, lambda o: left_z(o).start())

    def right_z(quarter):
        blocks = pl.ds(wrap(x + quarter, X) * CORE, CORE)
        return remote(right_out.at[blocks], right_row.at[blocks], rz_send.at[quarter], rz_recv.at[quarter],
                      row * XC + xc, t)

    @pl.when(hop != 0)
    def _():
        lax.fori_loop(0, X, lambda quarter, carry: (right_z(quarter).start(), carry)[1], 0)

    @pl.when(hop == 0)
    def _():
        def here(quarter, carry):
            blocks = pl.ds(wrap(x + quarter, X) * CORE, CORE)
            pltpu.make_async_copy(right_out.at[blocks], right_row.at[blocks], rz_recv.at[quarter]).start()
            return carry

        lax.fori_loop(0, X, here, 0)

    l_sae.wait()
    monitored = sae.shape[0]
    chooser = jnp.where(
        lax.broadcasted_iota(jnp.int32, (monitored, Q), 0) == feat_ref[...], 1.0, 0.0
    ).astype(bf16)
    l_bout.wait()
    wide = 384
    b_mine[...] = jnp.zeros_like(b_mine)

    def b_step(n, carry):
        columns = pl.ds(pl.multiple_of(n * wide, 128), wide)
        outputs = lax.dot_general(
            chooser, sae[:, columns], FIRST_ROWS, preferred_element_type=f32
        ).astype(bf16)
        b_mine[...] += lax.dot_general(
            outputs, bout[:, columns], LAST_COLUMNS, preferred_element_type=f32
        )
        return carry

    lax.fori_loop(0, DOUT // TENSOR // wide, b_step, 0)
    for n in range(TENSOR):
        b_part[n, :, 0:J] = b_mine[8 * n:8 * (n + 1), :]
    spread(TENSOR, t, lambda o: b_part.at[o], b_recv, b_send, b_rsem, in_t)
    b_recv[t] = b_part[t]

    l_acts.wait()
    context = acts.shape[1]
    picker = jnp.where(
        lax.broadcasted_iota(jnp.int32, (context, Q), 0) == pos_ref[...], 1.0, 0.0
    ).astype(bf16)
    inputs = jnp.dot(acts[...], picker, preferred_element_type=f32).astype(bf16)
    l_bin.wait()
    a_mine = lax.dot_general(inputs, bin_[...], FIRST_ROWS, preferred_element_type=f32)
    for n in range(XC):
        a_part[n] = a_mine[8 * n:8 * (n + 1)]
    spread(XC, xc, lambda o: a_part.at[o], a_xc, a_send, a_recv, in_xc)
    a_xc[xc] = a_part[xc]

    collect(ZH, zh, lambda o: e_mine, e_z, ez_send, ez_recv)
    e_sum[...] = total_of(e_z, ZH)
    spread(XC, xc, lambda o: e_sum, e_xc, e_send, e_recv, in_xc)
    e_xc[xc] = e_sum[...]

    def left_x(o):
        return remote(left.at[:, x, core], left.at[:, x, core], lx_send.at[o], lx_recv.at[x],
                      zh * XC + o * CORE + core, t)

    def left_core(o):
        return remote(left.at[:, o, core], left.at[:, o, core], lc_send.at[o], lc_recv.at[o],
                      zh * XC + x * CORE + (1 - core), t)

    others(ZH, zh, lambda o: remote(
        left.at[o, x, core], left.at[o, x, core], lz_send.at[o], lz_recv.at[o], d, t).wait_recv())
    others(X, x, lambda o: left_x(o).start())
    left_core(x).start()

    def right_x(o):
        return remote(right_row.at[o], right.at[column_seq], r_send.at[o], r_recv.at[column_seq],
                      zh * XC + o, t)

    def right_quarter(quarter):
        right_z(quarter).wait_recv()

        def one(c, carry):
            o = wrap(x + quarter, X) * CORE + c

            @pl.when(o != xc)
            def _():
                right_x(o).start()

            @pl.when(o == xc)
            def _():
                pltpu.make_async_copy(right_row.at[o], right.at[column_seq], r_recv.at[column_seq]).start()

            return carry

        lax.fori_loop(0, CORE, one, 0)

    def seq_of(k):
        g = jnp.where(k >= 16, jnp.where(k >= 24, 3, 2), jnp.where(k >= 8, 1, 0))
        m = k - 8 * g
        off = jnp.where(g == 0, 0, jnp.where(g == 3, 2, jnp.where((g == 1) == (m < 4), 1, 3)))
        pair = half_of(m)
        sx, sc = wrap(x - pair + X, X), m - 2 * pair
        return low_two(zh + wrap(y + off, Y) - sx - 2 * sc - zl + 2 * Y), sx, sc

    def flat(s):
        return (s[0] * X + s[1]) * CORE + s[2]

    def right_wait(s):
        remote(right.at[s], right.at[s], y_again.at[0], r_recv.at[s], d, t).wait_recv()

    def to_plane(s, off, sem):
        return remote(right.at[s], right.at[s], sem, r_recv.at[s], d, wrap(y + off, Y) * ZL + zl)

    def own(m, carry):
        s = flat(seq_of(m))
        right_wait(s)
        to_plane(s, 1, y_send.at[0, m]).start()
        to_plane(s, 3, y_send.at[1, m]).start()
        return carry

    right_quarter(0)
    right_quarter(1)

    collect(XC, xc, lambda o: a_part.at[o], a_xc, a_send, a_recv)
    a_mid[...] = total_of(a_xc, XC)
    spread(ZH, zh, lambda o: a_mid, a_z, az_send, az_recv, in_zh)
    a_z[zh] = a_mid[...]

    collect(TENSOR, t, lambda o: b_part.at[o], b_recv, b_send, b_rsem)
    b_sum[...] = total_of(b_recv, TENSOR)
    spread(TENSOR, t, lambda o: b_sum, b_all, bg_send, bg_recv, in_t)
    b_all[t] = b_sum[...]

    lax.fori_loop(0, 2, own, 0)
    right_quarter(2)

    collect(XC, xc, lambda o: e_sum, e_xc, e_send, e_recv)
    e_mid[...] = total_of(e_xc, XC)
    spread(TENSOR, t, lambda o: e_mid, e_t, et_send, et_recv, in_t)
    e_t[t] = e_mid[...]

    lax.fori_loop(2, 4, own, 0)
    right_quarter(3)

    collect(ZH, zh, lambda o: a_mid, a_z, az_send, az_recv)
    a_sum[...] = total_of(a_z, ZH) * (1.0 / math.sqrt(DIN * DOUT * R))
    spread(XC, xc, lambda o: a_sum, a_all, ag_send, ag_recv, in_xc)
    a_all[xc] = a_sum[...]

    def left_x_wait(o):
        remote(left.at[:, o, core], left.at[:, o, core], lx_send.at[o], lx_recv.at[o], d, t).wait_recv()
        left_core(o).start()

    others(X, x, left_x_wait)
    lax.fori_loop(4, 6, own, 0)

    collect(TENSOR, t, lambda o: e_mid, e_t, et_send, et_recv)
    shift = damping * (jnp.sum(total_of(e_t, TENSOR)) / (DIN * DOUT))

    def invert(n, carry):
        some = pl.ds(pl.multiple_of(n * 96, 8), 96)
        inv[some, :] = 1.0 / (inv[some, :] + shift)
        return carry

    lax.fori_loop(0, J // 96, invert, 0)

    collect(TENSOR, t, lambda o: b_sum, b_all, bg_send, bg_recv)
    for n in range(TENSOR // 2):
        pair = jnp.concatenate([b_all[2 * n], b_all[2 * n + 1]], axis=0)
        b_lo[16 * n:16 * (n + 1), :] = pair.astype(bf16)[:, 0:J]

    lax.fori_loop(6, 8, own, 0)

    def left_core_wait(o, carry):
        remote(left.at[:, o, 1 - core], left.at[:, o, 1 - core], lc_send.at[o], lc_recv.at[o], d, t).wait_recv()
        return carry

    lax.fori_loop(0, X, left_core_wait, 0)

    collect(XC, xc, lambda o: a_sum, a_all, ag_send, ag_recv)
    for n in range(XC):
        a_full[8 * n:8 * (n + 1), :] = a_all[n]

    def ready(part):
        def arrived(k, carry):
            right_wait(flat(seq_of(k)))
            return carry

        def arrived_and_on(k, carry):
            s = flat(seq_of(k))
            right_wait(s)
            m = k - 8
            to_plane(s, jnp.where(m < 4, 3, 1), y_again.at[m]).start()
            return carry

        first = part * 4

        @pl.when(jnp.logical_and(part >= 2, part < 4))
        def _():
            lax.fori_loop(first, first + 4, arrived_and_on, 0)

        @pl.when(part >= 4)
        def _():
            lax.fori_loop(first, first + 4, arrived, 0)

    def cross(s, slot):
        wide = lax.dot_general(
            right[flat(s), :, 0:J], left[s[0], s[1], s[2]], FIRST_ROWS, preferred_element_type=f32
        )
        damped[slot] = (wide * inv[...]).astype(bf16)

    def project(slot):
        part = jnp.dot(b_lo[...], damped[slot], preferred_element_type=f32) * a_full[...]
        row = part[:, 0:128]
        for n in range(1, I // 128):
            row = row + part[:, n * 128:(n + 1) * 128]
        rows[slot] = row

    def score(of, slot):
        row = jnp.sum(rows[slot], axis=1, keepdims=True)
        lane = lax.broadcasted_iota(jnp.int32, (Q, 128), 1)
        scores[...] = jnp.where(lane == of, row, scores[...])

    def step(k, before, slot):
        s = seq_of(k)
        cross(s, slot)
        project(1 - slot)
        score(before[0], slot)
        return before[1], flat(s)

    scores[...] = jnp.zeros_like(scores)
    rows[...] = jnp.zeros_like(rows)
    damped[1] = jnp.zeros((J, I), bf16)

    def eighth(part, before):
        ready(part)

        def two(h, before):
            before = step(part * 4 + 2 * h, before, 0)
            return step(part * 4 + 2 * h + 1, before, 1)

        return lax.fori_loop(0, 2, two, before)

    before = lax.fori_loop(0, SEQS // 4, eighth, (-1, -1))
    project(1)
    score(before[0], 0)
    score(before[1], 1)

    by_seq = scores[...].T
    for n in range(ZH):
        f_part[n, :, 0:Q] = by_seq[8 * n:8 * (n + 1), :]
        f_part[n, :, Q:128] = jnp.zeros((8, 128 - Q), f32)
    spread(ZH, zh, lambda o: f_part.at[o], f_z, fz_send, fz_recv, in_zh)
    f_z[zh] = f_part[zh]
    collect(ZH, zh, lambda o: f_part.at[o], f_z, fz_send, fz_recv)
    f_mid[...] = (f_z[0] + f_z[1]) + (f_z[2] + f_z[3])
    spread(XC, xc, lambda o: f_mid, f_xc, fx_send, fx_recv, in_xc)
    f_xc[xc] = f_mid[...]
    collect(XC, xc, lambda o: f_mid, f_xc, fx_send, fx_recv)
    total = f_xc[0]
    for n in range(1, XC):
        total = total + f_xc[n]
    f_last[...] = total
    spread(TENSOR, t, lambda o: f_last, f_t, ft_send, ft_recv, in_t)
    f_t[t] = f_last[...]

    @pl.when(hop != 0)
    def _():
        lax.fori_loop(0, X, lambda quarter, carry: (right_z(quarter).wait_send(), carry)[1], 0)

    others(XC, xc, lambda o: right_x(o).wait_send())

    def sent_y(m, carry):
        to_plane(0, 1, y_send.at[0, m]).wait_send()
        to_plane(0, 1, y_send.at[1, m]).wait_send()
        to_plane(0, 1, y_again.at[m]).wait_send()
        return carry

    lax.fori_loop(0, 8, sent_y, 0)
    drain(TENSOR, t, lambda o: b_part.at[o], b_recv, b_send, b_rsem)
    drain(TENSOR, t, lambda o: b_sum, b_all, bg_send, bg_recv)
    drain(ZH, zh, lambda o: e_mine, e_z, ez_send, ez_recv)
    drain(XC, xc, lambda o: e_sum, e_xc, e_send, e_recv)
    drain(TENSOR, t, lambda o: e_mid, e_t, et_send, et_recv)
    drain(XC, xc, lambda o: a_part.at[o], a_xc, a_send, a_recv)
    drain(ZH, zh, lambda o: a_mid, a_z, az_send, az_recv)
    drain(XC, xc, lambda o: a_sum, a_all, ag_send, ag_recv)
    drain(ZH, zh, lambda o: f_part.at[o], f_z, fz_send, fz_recv)
    drain(XC, xc, lambda o: f_mid, f_xc, fx_send, fx_recv)
    others(ZH, zh, lambda o: left_z(o).wait_send())
    others(X, x, lambda o: left_x(o).wait_send())

    def sent_left_core(o, carry):
        left_core(o).wait_send()
        return carry

    lax.fori_loop(0, X, sent_left_core, 0)

    collect(TENSOR, t, lambda o: f_last, f_t, ft_send, ft_recv)
    total = f_t[0]
    for n in range(1, TENSOR):
        total = total + f_t[n]
    f_last_row = jnp.sum(
        jnp.where(lax.broadcasted_iota(jnp.int32, (8, 128), 0) == xc, total, 0.0), axis=0, keepdims=True
    )
    out_ref[...] = f_last_row[:, 0:Q]
    drain(TENSOR, t, lambda o: f_last, f_t, ft_send, ft_recv)


def on_device(
    query_acts, query_pos, query_feat, sae_enc, basis_in, basis_out, eigvals, train_in, train_out
):
    context = query_acts.shape[0]
    monitored = sae_enc.shape[0]
    vmem = pltpu.VMEM
    dma = pltpu.SemaphoreType.DMA
    scratch = [
        vmem((DIN // DP, context), bf16), vmem((monitored, DOUT // TENSOR), bf16),
        vmem((DIN // DP, I), bf16), vmem((J, DOUT // TENSOR), bf16), vmem((J, I), f32),
        vmem((R, DOUT), bf16),
        vmem((XC, R, JP), bf16), vmem((XC, R, JP), bf16), vmem((SEQS, R, JP), bf16), vmem((ZH, X, CORE, R, I), bf16),
        vmem((Q, J), f32), vmem((TENSOR, 8, JP), f32), vmem((TENSOR, 8, JP), f32), vmem((8, JP), f32),
        vmem((TENSOR, 8, JP), f32), vmem((Q, J), bf16),
        vmem((8, 128), f32), vmem((ZH, 8, 128), f32), vmem((8, 128), f32), vmem((XC, 8, 128), f32),
        vmem((8, 128), f32), vmem((TENSOR, 8, 128), f32),
        vmem((XC, 8, I), f32), vmem((XC, 8, I), f32), vmem((8, I), f32), vmem((ZH, 8, I), f32),
        vmem((8, I), f32), vmem((XC, 8, I), f32), vmem((Q, I), f32),
        vmem((2, J, I), bf16), vmem((2, Q, 128), f32), vmem((Q, 128), f32),
        vmem((ZH, 8, 128), f32), vmem((ZH, 8, 128), f32), vmem((8, 128), f32),
        vmem((XC, 8, 128), f32), vmem((8, 128), f32), vmem((TENSOR, 8, 128), f32),
        dma((7,)), dma((X,)), dma((X,)), dma((XC,)), dma((SEQS,)), dma((2, 8)), dma((8,)),
        dma((ZH,)), dma((ZH,)), dma((X,)), dma((X,)), dma((X,)), dma((X,)),
        dma((TENSOR,)), dma((TENSOR,)), dma((TENSOR,)), dma((TENSOR,)),
        dma((ZH,)), dma((ZH,)), dma((XC,)), dma((XC,)), dma((TENSOR,)), dma((TENSOR,)),
        dma((XC,)), dma((XC,)), dma((ZH,)), dma((ZH,)), dma((XC,)), dma((XC,)),
        dma((ZH,)), dma((ZH,)), dma((XC,)), dma((XC,)), dma((TENSOR,)), dma((TENSOR,)),
    ]
    anywhere = pl.BlockSpec(memory_space=pl.ANY)
    inside = pl.BlockSpec(memory_space=pltpu.VMEM)
    return pl.pallas_call(
        kernel,
        out_shape=jax.ShapeDtypeStruct((1, Q), f32),
        in_specs=[inside, inside] + [anywhere] * 7,
        out_specs=inside,
        scratch_shapes=scratch,
        compiler_params=pltpu.CompilerParams(
            collective_id=0, has_side_effects=True, vmem_limit_bytes=56 << 20
        ),
        name="influence",
    )(
        query_pos.reshape(1, Q), query_feat.reshape(1, Q), query_acts.T, sae_enc, basis_in, basis_out.T,
        eigvals.T, train_in.reshape(R, I), train_out.reshape(R, DOUT),
    ).reshape(Q, 1)


def solution(mesh):
    in_specs = (
        P(None, "dp"),
        P(),
        P(),
        P(None, "tensor"),
        P("dp", "tensor"),
        P("tensor", "dp"),
        P("tensor", "dp"),
        P("dp", None, "tensor"),
        P("dp", None, None),
    )
    out_specs = P(None, "dp")
    return jax.shard_map(
        on_device, mesh=mesh, in_specs=in_specs, out_specs=out_specs, check_vma=False
    )
```

time: 103 us -> 77.6 us (0.75)
  local copies, waits for them, and re-layouts: 15.7 us -> 1.19 us
  Pallas kernels: 87.1 us -> 76.3 us
    unnamed x3 -> x1, local copies, waits for them, and re-layouts: 14.4 us -> 1.19 us
    pallas_call x1, Pallas kernels: 87.1 us -> 76.3 us  [on_device(): pl.pallas_call(kernel, out_shape=jax.ShapeDtypeStruct((1, Q), f32), in_sp...]
    pallas_call x1 -> x0, local copies, waits for them, and re-layouts: 1.34 us -> none  [on_device(): pl.pallas_call(kernel, out_shape=jax.ShapeDtypeStruct((Q, 1), f32), in_sp...]
where the time goes in v2:
time: 77.6 us; the launch traced here: 77.5 us
  Pallas kernels  76.3 us (98%)
  local copies, waits for them, and re-layouts  1.19 us (2%)
    pallas_call x1, Pallas kernels, on_device(): pl.pallas_call(kernel, out_shape=jax.ShapeDtypeStruct((1, Q), f32), in_sp...  76.3 us

profile of v2, /device:TPU:1, one launch (start us, length us, event | category | flops | bytes accessed | tf_op | source)
XLA Modules:
  0.0 77.5 jit_solution(16207222397244000422)
XLA Ops:
  0.0 76.3 %influence.1 = f32[1,64]{1,0:T(1,128)} custom-call(s32[1,64]{1,0:T(1,128)} %bitcast.13, s32[1,64]{1,0:T(1,128)} %bitcast.14, bf16[160,1024]{1,0:T(8,128)(2,1)} %bitcast.11, bf16[128,3456]{1,0:T(8,128)(2,1)} %sae_hbm.1, bf16[160,640]{1,0:T(8,128)(2,1)} %bin_hbm.1, bf16[864,3456]{1,0:T(8,128)(2,1)} %bitcast.8, f32[864,640]{1,0:T(8,128)} %bitcast.9, ...), custom_call_target="tpu_custom_call" | custom-call | tf_op jit(solution)/shard_map/influence/pallas_call | solution.py:503
  76.3 1.2 %copy.11 = f32[64,1]{0,1:T(1,128)} copy(f32[64,1]{0,1:T(1,128)} %bitcast.15) | data formatting | bytes 512

commit v3 on v2

--- a/solution.py
+++ b/solution.py
@@ -124,7 +124,14 @@
     def low_two(v):
         return wrap(wrap(v, 8), 4)
 
-    hop = low_two(x + 2 * core + zl - y + Y)
+    odd_zh = zh - 2 * half_of(zh)
+
+    def hop_of(sx, sc, plane):
+        off = low_two(sx + jnp.where(sc == zl, 0, 1) + 2 * zl - plane + Y)
+        flip = jnp.logical_and(odd_zh == 1, jnp.logical_or(off == 0, off == 2))
+        return wrap(off + jnp.where(flip, 2, 0), ZH)
+
+    hop = hop_of(x, core, y)
     row = wrap(zh + hop, ZH)
     column_seq = wrap(zh - hop + ZH, ZH) * XC + xc
 
@@ -166,18 +173,21 @@
         return remote(right_out.at[blocks], right_row.at[blocks], rz_send.at[quarter], rz_recv.at[quarter],
                       row * XC + xc, t)
 
-    @pl.when(hop != 0)
-    def _():
-        lax.fori_loop(0, X, lambda quarter, carry: (right_z(quarter).start(), carry)[1], 0)
-
-    @pl.when(hop == 0)
-    def _():
-        def here(quarter, carry):
-            blocks = pl.ds(wrap(x + quarter, X) * CORE, CORE)
-            pltpu.make_async_copy(right_out.at[blocks], right_row.at[blocks], rz_recv.at[quarter]).start()
-            return carry
-
-        lax.fori_loop(0, X, here, 0)
+    def right_z_start(first, last):
+        @pl.when(hop != 0)
+        def _():
+            lax.fori_loop(first, last, lambda quarter, carry: (right_z(quarter).start(), carry)[1], 0)
+
+        @pl.when(hop == 0)
+        def _():
+            def here(quarter, carry):
+                blocks = pl.ds(wrap(x + quarter, X) * CORE, CORE)
+                pltpu.make_async_copy(right_out.at[blocks], right_row.at[blocks], rz_recv.at[quarter]).start()
+                return carry
+
+            lax.fori_loop(first, last, here, 0)
+
+    right_z_start(0, 2)
 
     l_sae.wait()
     monitored = sae.shape[0]
@@ -217,6 +227,8 @@
     spread(XC, xc, lambda o: a_part.at[o], a_xc, a_send, a_recv, in_xc)
     a_xc[xc] = a_part[xc]
 
+    right_z_start(2, X)
+
     collect(ZH, zh, lambda o: e_mine, e_z, ez_send, ez_recv)
     e_sum[...] = total_of(e_z, ZH)
     spread(XC, xc, lambda o: e_sum, e_xc, e_send, e_recv, in_xc)
@@ -263,7 +275,7 @@
         off = jnp.where(g == 0, 0, jnp.where(g == 3, 2, jnp.where((g == 1) == (m < 4), 1, 3)))
         pair = half_of(m)
         sx, sc = wrap(x - pair + X, X), m - 2 * pair
-        return low_two(zh + wrap(y + off, Y) - sx - 2 * sc - zl + 2 * Y), sx, sc
+        return wrap(zh - hop_of(sx, sc, wrap(y + off, Y)) + ZH, ZH), sx, sc
 
     def flat(s):
         return (s[0] * X + s[1]) * CORE + s[2]
@@ -294,14 +306,13 @@
     spread(TENSOR, t, lambda o: b_sum, b_all, bg_send, bg_recv, in_t)
     b_all[t] = b_sum[...]
 
-    lax.fori_loop(0, 2, own, 0)
-    right_quarter(2)
-
     collect(XC, xc, lambda o: e_sum, e_xc, e_send, e_recv)
     e_mid[...] = total_of(e_xc, XC)
     spread(TENSOR, t, lambda o: e_mid, e_t, et_send, et_recv, in_t)
     e_t[t] = e_mid[...]
 
+    lax.fori_loop(0, 2, own, 0)
+    right_quarter(2)
     lax.fori_loop(2, 4, own, 0)
     right_quarter(3)
 

time: 77.6 us -> 73.6 us (0.948)
  Pallas kernels: 76.3 us -> 72.3 us
    pallas_call x1, Pallas kernels: 76.3 us -> 72.3 us  [on_device(): pl.pallas_call(kernel, out_shape=jax.ShapeDtypeStruct((1, Q), f32), in_sp...]
where the time goes in v3:
time: 73.6 us; the launch traced here: 73.5 us
  Pallas kernels  72.3 us (98%)
  local copies, waits for them, and re-layouts  1.19 us (2%)
    pallas_call x1, Pallas kernels, on_device(): pl.pallas_call(kernel, out_shape=jax.ShapeDtypeStruct((1, Q), f32), in_sp...  72.3 us

profile of v3, /device:TPU:1, one launch (start us, length us, event | category | flops | bytes accessed | tf_op | source)
XLA Modules:
  0.0 73.5 jit_solution(5064584981469588283)
XLA Ops:
  0.0 72.3 %influence.1 = f32[1,64]{1,0:T(1,128)} custom-call(s32[1,64]{1,0:T(1,128)} %bitcast.13, s32[1,64]{1,0:T(1,128)} %bitcast.14, bf16[160,1024]{1,0:T(8,128)(2,1)} %bitcast.11, bf16[128,3456]{1,0:T(8,128)(2,1)} %sae_hbm.1, bf16[160,640]{1,0:T(8,128)(2,1)} %bin_hbm.1, bf16[864,3456]{1,0:T(8,128)(2,1)} %bitcast.8, f32[864,640]{1,0:T(8,128)} %bitcast.9, ...), custom_call_target="tpu_custom_call" | custom-call | tf_op jit(solution)/shard_map/influence/pallas_call | solution.py:514
  72.3 1.2 %copy.11 = f32[64,1]{0,1:T(1,128)} copy(f32[64,1]{0,1:T(1,128)} %bitcast.15) | data formatting | bytes 512

commit v4 on v3

--- a/solution.py
+++ b/solution.py
@@ -413,7 +413,7 @@
             before = step(part * 4 + 2 * h, before, 0)
             return step(part * 4 + 2 * h + 1, before, 1)
 
-        return lax.fori_loop(0, 2, two, before)
+        return lax.fori_loop(0, 2, two, before, unroll=True)
 
     before = lax.fori_loop(0, SEQS // 4, eighth, (-1, -1))
     project(1)

time: 73.6 us -> 71.8 us (0.976)
  Pallas kernels: 72.3 us -> 70.5 us
    pallas_call x1, Pallas kernels: 72.3 us -> 70.5 us  [on_device(): pl.pallas_call(kernel, out_shape=jax.ShapeDtypeStruct((1, Q), f32), in_sp...]
where the time goes in v4:
time: 71.8 us; the launch traced here: 71.7 us
  Pallas kernels  70.5 us (98%)
  local copies, waits for them, and re-layouts  1.19 us (2%)
    pallas_call x1, Pallas kernels, on_device(): pl.pallas_call(kernel, out_shape=jax.ShapeDtypeStruct((1, Q), f32), in_sp...  70.5 us

profile of v4, /device:TPU:1, one launch (start us, length us, event | category | flops | bytes accessed | tf_op | source)
XLA Modules:
  0.0 71.7 jit_solution(6845254998311022292)
XLA Ops:
  0.0 70.5 %influence.1 = f32[1,64]{1,0:T(1,128)} custom-call(s32[1,64]{1,0:T(1,128)} %bitcast.13, s32[1,64]{1,0:T(1,128)} %bitcast.14, bf16[160,1024]{1,0:T(8,128)(2,1)} %bitcast.11, bf16[128,3456]{1,0:T(8,128)(2,1)} %sae_hbm.1, bf16[160,640]{1,0:T(8,128)(2,1)} %bin_hbm.1, bf16[864,3456]{1,0:T(8,128)(2,1)} %bitcast.8, f32[864,640]{1,0:T(8,128)} %bitcast.9, ...), custom_call_target="tpu_custom_call" | custom-call | tf_op jit(solution)/shard_map/influence/pallas_call | solution.py:514
  70.5 1.2 %copy.11 = f32[64,1]{0,1:T(1,128)} copy(f32[64,1]{0,1:T(1,128)} %bitcast.15) | data formatting | bytes 512
